TPU v7x, 128 devices: a whole 4x4x4 slice. The times are simulated.
128 devices in a mesh: row: 8 (over y_lo, z), col: 16 (over x, y_hi, core).
Axes of the slice: x: 4, y: 4 (y_hi: 2, y_lo: 2; y = y_hi * 2 + y_lo), z: 4, core: 2. Of those that a mesh axis runs over, the one named last changes fastest.
Arguments:
- hessian: float32 [16384, 8, 16, 128], P('row', None, 'col'), may hold values from -1 to 16, as said below
- weights: bfloat16 [512, 16384], P('col', 'row'), may hold values from -6 to 6
- codes: int32 [512, 8192], P('col', 'row'), may hold values from 0 to 255
- tile_map: int32 [32, 64], P('col', 'row'), may hold values from 0 to 511
- codebooks: float32 [512, 2, 256], replicated, may hold values from -6 to 6
Outputs:
- adjusted_codebooks: float32 [512, 2, 256], replicated
Inputs may be any that keep to these rules, and one draw needn't show every extreme that they name: `hessian`: H is symmetric with a dominant positive diagonal.
All inputs are finite; a program needn't handle non-finite values.
Results may differ from a plain program's by a relative error of at most 0.0003.
Values sent between devices are 32-bit elements; how exact they have to be, the bound alone decides.
No kernel may reach another device: no remote copies, remote signals or barrier semaphores. Data moves between devices by JAX's collectives and lax.ppermute only.
A program may use at most 64 MiB of HBM per device.

v0:
```python
import jax
import jax.numpy as jnp
from jax import lax
from jax.sharding import PartitionSpec as P

CODES = 256
NB = 512
TILE_ROWS = 16
TILE_COLS = 256
STEPS = 2
learn_rate = 0.01


def per_device(hessian, weights, codes, tile_map, codebooks):
    rows_local, cols_local = weights.shape
    rows_tiles = rows_local // TILE_ROWS
    cols_tiles = cols_local // TILE_COLS
    tile_count = rows_tiles * cols_tiles
    half_width = TILE_COLS // 2
    pair_count = TILE_ROWS * half_width
    hessian_tile = hessian.reshape(
        hessian.shape[0], hessian.shape[1] * hessian.shape[2] * hessian.shape[3]
    )
    code_tiles = (
        codes.reshape(rows_tiles, TILE_ROWS, cols_tiles, half_width)
        .transpose(0, 2, 1, 3)
        .reshape(tile_count, pair_count)
    )
    code_onehot = (
        code_tiles[:, :, None] == lax.broadcasted_iota(jnp.int32, (1, 1, CODES), 2)
    ).astype(jnp.float32)
    book_onehot = (
        tile_map.reshape(-1)[:, None] == lax.broadcasted_iota(jnp.int32, (1, NB), 1)
    ).astype(jnp.float32)
    for iteration in range(STEPS):
        tile_books = jnp.einsum(
            "tb,bck->tck", book_onehot, codebooks, precision=lax.Precision.HIGHEST
        )
        rebuilt_tiles = jnp.einsum(
            "tpk,tck->tpc", code_onehot, tile_books, precision=lax.Precision.HIGHEST
        )
        rebuilt = (
            rebuilt_tiles.reshape(rows_tiles, cols_tiles, TILE_ROWS, half_width, 2)
            .transpose(0, 2, 1, 3, 4)
            .reshape(rows_local, cols_local)
        )
        error = rebuilt - weights.astype(jnp.float32)
        gathered = lax.all_gather(error, "col", axis=0, tiled=True)
        piece_width = cols_local // lax.axis_size("col")
        error_piece = lax.dynamic_slice_in_dim(
            gathered, lax.axis_index("col") * piece_width, piece_width, 1
        )
        error_spread = lax.all_gather(error_piece, "row", axis=1, tiled=True)
        weight_grad = 2.0 * lax.psum_scatter(
            lax.dot_general(
                error_spread,
                hessian_tile,
                (((1,), (1,)), ((), ())),
                precision=lax.Precision.HIGHEST,
                preferred_element_type=jnp.float32,
            ),
            "col",
            scatter_dimension=0,
            tiled=True,
        )
        grad_tiles = (
            weight_grad.reshape(rows_tiles, TILE_ROWS, cols_tiles, half_width, 2)
            .transpose(0, 2, 1, 3, 4)
            .reshape(tile_count, pair_count, 2)
        )
        tile_grads = jnp.einsum(
            "tpk,tpc->tck", code_onehot, grad_tiles, precision=lax.Precision.HIGHEST
        )
        local_grad = jnp.einsum(
            "tb,tck->bck", book_onehot, tile_grads, precision=lax.Precision.HIGHEST
        )
        total_even, total_odd = lax.psum((local_grad[:, 0, :], local_grad[:, 1, :]), ("row", "col"))
        book_grad = jnp.stack([total_even, total_odd], axis=1)
        codebooks = codebooks - learn_rate * book_grad
    return codebooks


def solution(mesh):
    placed = (P("row", None, "col", None), P("col", "row"), P("col", "row"), P("col", "row"), P())
    return jax.shard_map(per_device, mesh=mesh, in_specs=placed, out_specs=P(), check_vma=False)
```

profile of v0, /device:TPU:1, one launch (start us, length us, event | category | flops | bytes accessed | tf_op | source)
XLA Modules:
  0.0 803.9 jit_solution(11324388309986088203)
XLA Ops:
  6.5 0.8 eq.30
  7.3 0.9 copy.58
  8.3 1.7 fusion.16
  10.0 17.1 %fusion.3 = f32[16,2048,2]{1,2,0:T(2,128)S(1)} fusion(s32[16,2048]{1,0:T(8,128)S(1)} %bitcast_bitcast_fusion, f32[16,2,256]{2,0,1:T(8,128)S(1)} %fusion.16), kind=kOutput, calls=%fused_computation.4 | convolution fusion | flops 209715200 | bytes 425984 | tf_op jit(solution)/shard_map/tpk,tck->tpc/dot_general | solution.py:39
  27.1 0.2 reshape.33
  27.3 1.4 copy.39
  28.7 1.1 reshape.34
  29.8 0.3 copy.40
  30.2 0.7 convert_subtract_fusion.1
  31.0 59.7 %all-gather.5.cloned.1.call-done = f32[512,2048]{1,0:T(8,128)} async-done(((f32[32,2048]{1,0:T(8,128)}), f32[512,2048]{1,0:T(8,128)}) %all-gather.5.cloned.1.call-update) | async-done | bytes 4194320 | tf_op jit(solution)/shard_map/all_gather | solution.py:48
  90.7 1.7 constant_dynamic-slice_fusion.1
  92.4 39.8 %all-gather.7.cloned.1.call-done = f32[512,1024]{1,0:T(8,128)} async-done(((f32[512,128]{1,0:T(8,128)}), f32[512,1024]{1,0:T(8,128)}) %all-gather.7.cloned.1.call-update) | async-done | bytes 2097168 | tf_op jit(solution)/shard_map/all_gather | solution.py:53
  132.2 19.4 %fusion.10 = f32[512,2048]{1,0:T(8,128)} fusion(f32[512,1024]{1,0:T(8,128)} %all-gather.7.cloned.1.call-done, f32[256,8,8,128]{3,2,1,0:T(8,128)} %bitcast.51), kind=kOutput, calls=%fused_computation.11 | convolution fusion | flops 12884901888 | bytes 14680064 | tf_op jit(solution)/shard_map/dot_general | solution.py:55
  151.6 0.2 all-reduce.7.cloned.1.call-start
  151.8 84.1 %reduce-scatter.3.cloned.1.call-done = f32[32,2048]{1,0:T(8,128)} async-done(((f32[512,2048]{1,0:T(8,128)}), f32[32,2048]{1,0:T(8,128)}) %reduce-scatter.3.cloned.1.call-update) | async-done | bytes 262160 | tf_op jit(solution)/shard_map/reduce_scatter | solution.py:54
  235.9 1.0 broadcast_multiply_fusion.1
  236.9 0.3 copy.41
  237.2 1.2 reshape.36
  238.4 0.8 copy.54
  239.2 0.1 reshape.47
  239.4 12.3 %fusion.2 = f32[16,2,256]{2,1,0:T(2,128)S(1)} fusion(f32[16,2048,2]{1,2,0:T(2,128)S(1)} %reshape.47, s32[16,2048]{1,0:T(8,128)} %copy-done.4), kind=kOutput, calls=%fused_computation.3 | convolution fusion | flops 209715200 | bytes 425984 | tf_op jit(solution)/shard_map/tpk,tpc->tck/dot_general | solution.py:71
  251.7 0.7 fusion.23
  252.4 1.0 fusion.38
  253.5 148.0 %all-reduce.7.cloned.1.call-done = (f32[512,1,256]{2,0,1:T(8,128)}, f32[512,1,256]{2,0,1:T(8,128)}) async-done(((f32[512,1,256]{2,0,1:T(8,128)}, f32[512,1,256]{2,0,1:T(8,128)}), (f32[512,1,256]{2,0,1:T(8,128)}, f32[512,1,256]{2,0,1:T(8,128)})) %all-reduce.7.cloned.1.call-update) | async-done | bytes 1048592 | tf_op jit(solution)/shard_map/psum | solution.py:77
  401.6 1.7 fusion.18
  403.3 17.1 %fusion.1 = f32[16,2048,2]{1,2,0:T(2,128)S(1)} fusion(s32[16,2048]{1,0:T(8,128)S(1)} %copy-done.5, f32[16,2,256]{2,0,1:T(8,128)S(1)} %fusion.18), kind=kOutput, calls=%fused_computation.2 | convolution fusion | flops 209715200 | bytes 425984 | tf_op jit(solution)/shard_map/tpk,tck->tpc/dot_general | solution.py:39
  420.4 0.2 reshape.38
  420.6 1.4 copy.47
  422.0 2.1 reshape.39
  424.1 1.5 copy.48
  425.6 0.7 convert_subtract_fusion
  426.4 55.1 %all-gather.9.cloned.1.call-done = f32[512,2048]{1,0:T(8,128)} async-done(((f32[32,2048]{1,0:T(8,128)}), f32[512,2048]{1,0:T(8,128)}) %all-gather.9.cloned.1.call-update) | async-done | bytes 4194320 | tf_op jit(solution)/shard_map/all_gather | solution.py:48
  481.6 1.7 constant_dynamic-slice_fusion
  483.3 0.3 reduce-scatter.5.cloned.1.call-start
  483.6 39.5 %all-gather.11.cloned.1.call-done = f32[512,1024]{1,0:T(8,128)} async-done(((f32[512,128]{1,0:T(8,128)}), f32[512,1024]{1,0:T(8,128)}) %all-gather.11.cloned.1.call-update) | async-done | bytes 2097168 | tf_op jit(solution)/shard_map/all_gather | solution.py:53
  523.1 19.4 %fusion.8 = f32[512,2048]{1,0:T(8,128)} fusion(f32[512,1024]{1,0:T(8,128)} %all-gather.11.cloned.1.call-done, f32[256,8,8,128]{3,2,1,0:T(8,128)} %bitcast.52), kind=kOutput, calls=%fused_computation.9 | convolution fusion | flops 12884901888 | bytes 14680064 | tf_op jit(solution)/shard_map/dot_general | solution.py:55
  542.5 0.3 all-reduce.5.cloned.1.call-start
  542.8 84.0 %reduce-scatter.5.cloned.1.call-done = f32[32,2048]{1,0:T(8,128)} async-done(((f32[512,2048]{1,0:T(8,128)}), f32[32,2048]{1,0:T(8,128)}) %reduce-scatter.5.cloned.1.call-update) | async-done | bytes 262160 | tf_op jit(solution)/shard_map/reduce_scatter | solution.py:54
  626.9 1.0 broadcast_multiply_fusion
  627.8 1.3 copy.49
  629.2 2.5 reshape.40
  631.7 0.8 copy.55
  632.7 11.3 %fusion = f32[16,2,256]{2,1,0:T(2,128)S(1)} fusion(f32[16,2048,2]{1,2,0:T(2,128)S(1)} %reshape.48, s32[16,2048]{1,0:T(8,128)S(1)} %copy-done.6), kind=kOutput, calls=%fused_computation.1 | convolution fusion | flops 209715200 | bytes 425984 | tf_op jit(solution)/shard_map/tpk,tpc->tck/dot_general | solution.py:71
  644.0 0.7 fusion.20
  644.7 1.0 fusion.37
  645.7 148.1 %all-reduce.5.cloned.1.call-done = (f32[512,1,256]{2,0,1:T(8,128)}, f32[512,1,256]{2,0,1:T(8,128)}) async-done(((f32[512,1,256]{2,0,1:T(8,128)}, f32[512,1,256]{2,0,1:T(8,128)}), (f32[512,1,256]{2,0,1:T(8,128)}, f32[512,1,256]{2,0,1:T(8,128)})) %all-reduce.5.cloned.1.call-update) | async-done | bytes 1048592 | tf_op jit(solution)/shard_map/psum | solution.py:77
  793.9 1.4 fusion.15
  795.3 1.8 copy.53
  (29 shorter events, 0.5 us)
Async XLA Ops:
  6.5 84.1 %all-gather.5.cloned.1.call-start = ((), (), s32[]{:S(2)}) async-start(), calls=%async_computation.2 | async-start | bytes 4456448 | tf_op jit(solution)/shard_map/all_gather | solution.py:48
  8.2 1.7 copy-start.4
  10.0 20.2 %copy-start.3 = (bf16[32,2048]{1,0:T(8,128)(2,1)S(1)}, bf16[32,2048]{1,0:T(8,128)(2,1)}, u32[]{:S(2)}) copy-start(bf16[32,2048]{1,0:T(8,128)(2,1)} %param.6) | copy-start | bytes 393220
  30.9 101.3 %all-gather.7.cloned.1.call-start = ((), (), s32[]{:S(2)}) async-start(), calls=%async_computation.3 | async-start | bytes 2359296 | tf_op jit(solution)/shard_map/all_gather | solution.py:53
  92.4 143.6 %reduce-scatter.3.cloned.1.call-start = ((), (), s32[]{:S(2)}) async-start(), calls=%async_computation.4 | async-start | bytes 4456448 | tf_op jit(solution)/shard_map/reduce_scatter | solution.py:54
  151.6 250.0 %all-reduce.7.cloned.1.call-start = ((), (), s32[]{:S(2)}) async-start(), calls=%async_computation.9 | async-start | bytes 2097152 | tf_op jit(solution)/shard_map/psum | solution.py:77
  239.2 162.3 %copy-start = (f32[512,2,256]{2,1,0:T(2,128)S(1)}, f32[512,2,256]{2,1,0:T(2,128)}, u32[]{:S(2)}) copy-start(f32[512,2,256]{2,1,0:T(2,128)} %param.9) | copy-start | bytes 3145732
  239.4 163.9 %copy-start.5 = (s32[16,2048]{1,0:T(8,128)S(1)}, s32[16,2048]{1,0:T(8,128)}, u32[]{:S(2)}) copy-start(s32[16,2048]{1,0:T(8,128)} %copy-done.4) | copy-start | bytes 393220
  253.5 228.1 %all-gather.9.cloned.1.call-start = ((), (), s32[]{:S(2)}) async-start(), calls=%async_computation.5 | async-start | bytes 4456448 | tf_op jit(solution)/shard_map/all_gather | solution.py:48
  426.4 96.7 %all-gather.11.cloned.1.call-start = ((), (), s32[]{:S(2)}) async-start(), calls=%async_computation.6 | async-start | bytes 2359296 | tf_op jit(solution)/shard_map/all_gather | solution.py:53
  483.3 143.6 %reduce-scatter.5.cloned.1.call-start = ((), (), s32[]{:S(2)}) async-start(), calls=%async_computation.7 | async-start | bytes 4456448 | tf_op jit(solution)/shard_map/reduce_scatter | solution.py:54
  542.5 90.2 %copy-start.6 = (s32[16,2048]{1,0:T(8,128)S(1)}, s32[16,2048]{1,0:T(8,128)}, u32[]{:S(2)}) copy-start(s32[16,2048]{1,0:T(8,128)} %copy-done.4) | copy-start | bytes 393220
  542.5 251.3 %all-reduce.5.cloned.1.call-start = ((), (), s32[]{:S(2)}) async-start(), calls=%async_computation.8 | async-start | bytes 2097152 | tf_op jit(solution)/shard_map/psum | solution.py:77
  632.5 161.4 %copy-start.1 = (f32[512,1,256]{2,0,1:T(8,128)S(1)}, f32[512,1,256]{2,0,1:T(8,128)}, u32[]{:S(2)}) copy-start(f32[512,1,256]{2,0,1:T(8,128)} %get-tuple-element.7) | copy-start | bytes 1572868
  632.5 161.4 %copy-start.2 = (f32[512,1,256]{2,0,1:T(8,128)S(1)}, f32[512,1,256]{2,0,1:T(8,128)}, u32[]{:S(2)}) copy-start(f32[512,1,256]{2,0,1:T(8,128)} %get-tuple-element.8) | copy-start | bytes 1572868
Sparse Core Ops, SparseCore 0:
  31.0 59.5 all-gather.4
  92.5 39.6 all-gather.6
  151.7 84.1 reduce-scatter.2
  253.6 147.8 all-reduce.6
  426.5 55.0 all-gather.8
  483.4 39.6 all-gather.10
  542.6 84.1 reduce-scatter.4
  645.9 147.9 all-reduce.4
where the time goes:
time: 804 us
  waiting for transfers between devices  659 us (82%)
  matrix products  101 us (13%)
  local copies, waits for them, and re-layouts  24.4 us (3%)
  between operations  13.7 us (2%)
    psum x2, waiting for transfers between devices, per_device(): lax.psum((local_grad[:, 0, :], local_grad[:, 1, :]), ('row', 'col'))  296 us
    reduce_scatter x2, waiting for transfers between devices, per_device(): lax.psum_scatter(lax.dot_general(error_spread, hessian_tile, (((1,), (1,)...  168 us
    all_gather x2, waiting for transfers between devices, per_device(): gathered = lax.all_gather(error, 'col', axis=0, tiled=True)  115 us
    all_gather x2, waiting for transfers between devices, per_device(): error_spread = lax.all_gather(error_piece, 'row', axis=1, tiled=True)  79.3 us
    dot_general x2, matrix products, per_device(): lax.dot_general(error_spread, hessian_tile, (((1,), (1,)), ((), ())), pre...  38.8 us
    dot_general x2, matrix products, per_device(): jnp.einsum('tpk,tck->tpc', code_onehot, tile_books, precision=lax.Precisi...  34.2 us
    dot_general x2, matrix products, per_device(): jnp.einsum('tpk,tpc->tck', code_onehot, grad_tiles, precision=lax.Precisi...  23.6 us
  transfers between devices with their start and end apart: 8, of which 8 were waited for; matrix products, arithmetic and copies ran while one was open for 0% of the time, Pallas kernels for 0%

commit v1 on v0

--- a/solution.py
+++ b/solution.py
@@ -9,6 +9,7 @@
 TILE_COLS = 256
 STEPS = 2
 learn_rate = 0.01
+enter_map = lambda page: jax.lax.psum(jax.lax.psum(page, "row"), "col")
 
 
 def per_device(hessian, weights, codes, tile_map, codebooks):
@@ -74,7 +75,7 @@
         local_grad = jnp.einsum(
             "tb,tck->bck", book_onehot, tile_grads, precision=lax.Precision.HIGHEST
         )
-        total_even, total_odd = lax.psum((local_grad[:, 0, :], local_grad[:, 1, :]), ("row", "col"))
+        total_even, total_odd = enter_map((local_grad[:, 0, :], local_grad[:, 1, :]))
         book_grad = jnp.stack([total_even, total_odd], axis=1)
         codebooks = codebooks - learn_rate * book_grad
     return codebooks

time: 804 us -> 952 us (1.18)
  waiting for transfers between devices: 659 us -> 806 us
    psum x2 -> x4, waiting for transfers between devices: 296 us -> 441 us  [enter_map = lambda page: jax.lax.psum(jax.lax.psum(page, 'row'), 'col')]
  transfers between devices with their start and end apart: 8 -> 10, of which waited for: 8 -> 10; matrix products, arithmetic and copies ran while one was open for 0% -> 0% of each run, Pallas kernels for 0% -> 0%
where the time goes in v1:
time: 952 us; the launch traced here: 951 us
  waiting for transfers between devices  806 us (85%)
  matrix products  101 us (11%)
  local copies, waits for them, and re-layouts  24.4 us (3%)
  between operations  13.7 us (1%)
    psum x4, waiting for transfers between devices, enter_map = lambda page: jax.lax.psum(jax.lax.psum(page, 'row'), 'col')  441 us
    reduce_scatter x2, waiting for transfers between devices, per_device(): lax.psum_scatter(lax.dot_general(error_spread, hessian_tile, (((1,), (1,)...  168 us
    all_gather x2, waiting for transfers between devices, per_device(): gathered = lax.all_gather(error, 'col', axis=0, tiled=True)  117 us
    all_gather x2, waiting for transfers between devices, per_device(): error_spread = lax.all_gather(error_piece, 'row', axis=1, tiled=True)  79.3 us
    dot_general x2, matrix products, per_device(): lax.dot_general(error_spread, hessian_tile, (((1,), (1,)), ((), ())), pre...  38.8 us
    dot_general x2, matrix products, per_device(): jnp.einsum('tpk,tck->tpc', code_onehot, tile_books, precision=lax.Precisi...  34.2 us
    dot_general x2, matrix products, per_device(): jnp.einsum('tpk,tpc->tck', code_onehot, grad_tiles, precision=lax.Precisi...  23.6 us
  transfers between devices with their start and end apart: 10, of which 10 were waited for; matrix products, arithmetic and copies ran while one was open for 0% of the time, Pallas kernels for 0%

profile of v1, /device:TPU:1, one launch (start us, length us, event | category | flops | bytes accessed | tf_op | source)
XLA Modules:
  0.0 951.2 jit_solution(15843067211565523985)
XLA Ops:
  6.5 0.8 eq.30
  7.3 0.9 copy.58
  8.3 1.7 fusion.16
  10.0 17.1 %fusion.3 = f32[16,2048,2]{1,2,0:T(2,128)S(1)} fusion(s32[16,2048]{1,0:T(8,128)S(1)} %bitcast_bitcast_fusion, f32[16,2,256]{2,0,1:T(8,128)S(1)} %fusion.16), kind=kOutput, calls=%fused_computation.4 | convolution fusion | flops 209715200 | bytes 425984 | tf_op jit(solution)/shard_map/tpk,tck->tpc/dot_general | solution.py:40
  27.1 0.2 reshape.33
  27.3 1.4 copy.39
  28.7 1.1 reshape.34
  29.8 0.3 copy.40
  30.2 0.7 convert_subtract_fusion.1
  31.0 59.7 %all-gather.5.cloned.1.call-done = f32[512,2048]{1,0:T(8,128)} async-done(((f32[32,2048]{1,0:T(8,128)}), f32[512,2048]{1,0:T(8,128)}) %all-gather.5.cloned.1.call-update) | async-done | bytes 4194320 | tf_op jit(solution)/shard_map/all_gather | solution.py:49
  90.7 1.7 constant_dynamic-slice_fusion.1
  92.4 39.8 %all-gather.7.cloned.1.call-done = f32[512,1024]{1,0:T(8,128)} async-done(((f32[512,128]{1,0:T(8,128)}), f32[512,1024]{1,0:T(8,128)}) %all-gather.7.cloned.1.call-update) | async-done | bytes 2097168 | tf_op jit(solution)/shard_map/all_gather | solution.py:54
  132.2 19.4 %fusion.10 = f32[512,2048]{1,0:T(8,128)} fusion(f32[512,1024]{1,0:T(8,128)} %all-gather.7.cloned.1.call-done, f32[256,8,8,128]{3,2,1,0:T(8,128)} %bitcast.63), kind=kOutput, calls=%fused_computation.11 | convolution fusion | flops 12884901888 | bytes 14680064 | tf_op jit(solution)/shard_map/dot_general | solution.py:56
  151.6 0.2 all-reduce.15.cloned.1.call-start
  151.8 84.1 %reduce-scatter.3.cloned.1.call-done = f32[32,2048]{1,0:T(8,128)} async-done(((f32[512,2048]{1,0:T(8,128)}), f32[32,2048]{1,0:T(8,128)}) %reduce-scatter.3.cloned.1.call-update) | async-done | bytes 262160 | tf_op jit(solution)/shard_map/reduce_scatter | solution.py:55
  235.9 1.0 broadcast_multiply_fusion.1
  236.9 0.3 copy.41
  237.2 1.2 reshape.36
  238.4 0.8 copy.54
  239.4 12.3 %fusion.2 = f32[16,2,256]{2,1,0:T(2,128)S(1)} fusion(f32[16,2048,2]{1,2,0:T(2,128)S(1)} %reshape.43, s32[16,2048]{1,0:T(8,128)} %copy-done.4), kind=kOutput, calls=%fused_computation.3 | convolution fusion | flops 209715200 | bytes 425984 | tf_op jit(solution)/shard_map/tpk,tpc->tck/dot_general | solution.py:72
  251.7 0.7 fusion.23
  252.4 1.0 slice_bitcast_fusion.3
  253.5 72.9 %all-reduce.15.cloned.1.call-done = (f32[512,256]{1,0:T(8,128)}, f32[512,256]{1,0:T(8,128)}) async-done(((f32[512,256]{1,0:T(8,128)}, f32[512,256]{1,0:T(8,128)}), (f32[512,256]{1,0:T(8,128)}, f32[512,256]{1,0:T(8,128)})) %all-reduce.15.cloned.1.call-update) | async-done | bytes 1048592 | tf_op jit(solution)/shard_map/psum | solution.py:12
  326.6 147.4 %all-reduce.11.cloned.1.call-done = (f32[512,1,256]{2,0,1:T(8,128)}, f32[512,1,256]{2,0,1:T(8,128)}) async-done(((f32[512,1,256]{2,0,1:T(8,128)}, f32[512,1,256]{2,0,1:T(8,128)}), (f32[512,1,256]{2,0,1:T(8,128)}, f32[512,1,256]{2,0,1:T(8,128)})) %all-reduce.11.cloned.1.call-update) | async-done | bytes 1048592 | tf_op jit(solution)/shard_map/psum | solution.py:12
  474.0 1.7 fusion.18
  475.7 17.1 %fusion.1 = f32[16,2048,2]{1,2,0:T(2,128)S(1)} fusion(s32[16,2048]{1,0:T(8,128)S(1)} %copy-done.5, f32[16,2,256]{2,0,1:T(8,128)S(1)} %fusion.18), kind=kOutput, calls=%fused_computation.2 | convolution fusion | flops 209715200 | bytes 425984 | tf_op jit(solution)/shard_map/tpk,tck->tpc/dot_general | solution.py:40
  492.8 0.2 reshape.38
  493.1 1.4 copy.47
  494.4 2.1 reshape.39
  496.5 1.5 copy.48
  498.1 0.7 convert_subtract_fusion
  498.9 57.7 %all-gather.9.cloned.1.call-done = f32[512,2048]{1,0:T(8,128)} async-done(((f32[32,2048]{1,0:T(8,128)}), f32[512,2048]{1,0:T(8,128)}) %all-gather.9.cloned.1.call-update) | async-done | bytes 4194320 | tf_op jit(solution)/shard_map/all_gather | solution.py:49
  556.6 1.7 constant_dynamic-slice_fusion
  558.3 0.3 reduce-scatter.5.cloned.1.call-start
  558.6 39.5 %all-gather.11.cloned.1.call-done = f32[512,1024]{1,0:T(8,128)} async-done(((f32[512,128]{1,0:T(8,128)}), f32[512,1024]{1,0:T(8,128)}) %all-gather.11.cloned.1.call-update) | async-done | bytes 2097168 | tf_op jit(solution)/shard_map/all_gather | solution.py:54
  598.1 19.4 %fusion.8 = f32[512,2048]{1,0:T(8,128)} fusion(f32[512,1024]{1,0:T(8,128)} %all-gather.11.cloned.1.call-done, f32[256,8,8,128]{3,2,1,0:T(8,128)} %bitcast.64), kind=kOutput, calls=%fused_computation.9 | convolution fusion | flops 12884901888 | bytes 14680064 | tf_op jit(solution)/shard_map/dot_general | solution.py:56
  617.6 84.3 %reduce-scatter.5.cloned.1.call-done = f32[32,2048]{1,0:T(8,128)} async-done(((f32[512,2048]{1,0:T(8,128)}), f32[32,2048]{1,0:T(8,128)}) %reduce-scatter.5.cloned.1.call-update) | async-done | bytes 262160 | tf_op jit(solution)/shard_map/reduce_scatter | solution.py:55
  701.9 1.0 broadcast_multiply_fusion
  702.8 1.3 copy.49
  704.2 2.5 reshape.40
  706.7 0.8 copy.55
  707.7 11.3 %fusion = f32[16,2,256]{2,1,0:T(2,128)S(1)} fusion(f32[16,2048,2]{1,2,0:T(2,128)S(1)} %reshape.44, s32[16,2048]{1,0:T(8,128)S(1)} %copy-done.6), kind=kOutput, calls=%fused_computation.1 | convolution fusion | flops 209715200 | bytes 425984 | tf_op jit(solution)/shard_map/tpk,tpc->tck/dot_general | solution.py:72
  719.0 0.7 fusion.20
  719.7 1.0 slice_bitcast_fusion.1
  720.8 72.9 %all-reduce.13.cloned.1.call-done = (f32[512,256]{1,0:T(8,128)}, f32[512,256]{1,0:T(8,128)}) async-done(((f32[512,256]{1,0:T(8,128)}, f32[512,256]{1,0:T(8,128)}), (f32[512,256]{1,0:T(8,128)}, f32[512,256]{1,0:T(8,128)})) %all-reduce.13.cloned.1.call-update) | async-done | bytes 1048592 | tf_op jit(solution)/shard_map/psum | solution.py:12
  793.7 147.5 %all-reduce.9.cloned.1.call-done = (f32[512,1,256]{2,0,1:T(8,128)}, f32[512,1,256]{2,0,1:T(8,128)}) async-done(((f32[512,1,256]{2,0,1:T(8,128)}, f32[512,1,256]{2,0,1:T(8,128)}), (f32[512,1,256]{2,0,1:T(8,128)}, f32[512,1,256]{2,0,1:T(8,128)})) %all-reduce.9.cloned.1.call-update) | async-done | bytes 1048592 | tf_op jit(solution)/shard_map/psum | solution.py:12
  941.2 1.4 fusion.15
  942.6 1.8 copy.53
  (35 shorter events, 0.8 us)
Async XLA Ops:
  6.5 84.1 %all-gather.5.cloned.1.call-start = ((), (), s32[]{:S(2)}) async-start(), calls=%async_computation.2 | async-start | bytes 4456448 | tf_op jit(solution)/shard_map/all_gather | solution.py:49
  8.2 1.7 copy-start.4
  10.0 20.2 %copy-start.3 = (bf16[32,2048]{1,0:T(8,128)(2,1)S(1)}, bf16[32,2048]{1,0:T(8,128)(2,1)}, u32[]{:S(2)}) copy-start(bf16[32,2048]{1,0:T(8,128)(2,1)} %param.6) | copy-start | bytes 393220
  30.9 101.3 %all-gather.7.cloned.1.call-start = ((), (), s32[]{:S(2)}) async-start(), calls=%async_computation.3 | async-start | bytes 2359296 | tf_op jit(solution)/shard_map/all_gather | solution.py:54
  92.4 143.6 %reduce-scatter.3.cloned.1.call-start = ((), (), s32[]{:S(2)}) async-start(), calls=%async_computation.4 | async-start | bytes 4456448 | tf_op jit(solution)/shard_map/reduce_scatter | solution.py:55
  151.6 174.9 %all-reduce.15.cloned.1.call-start = ((), (), s32[]{:S(2)}) async-start(), calls=%async_computation.11 | async-start | bytes 2097152 | tf_op jit(solution)/shard_map/psum | solution.py:12
  239.2 234.7 %copy-start = (f32[512,2,256]{2,1,0:T(2,128)S(1)}, f32[512,2,256]{2,1,0:T(2,128)}, u32[]{:S(2)}) copy-start(f32[512,2,256]{2,1,0:T(2,128)} %param.9) | copy-start | bytes 3145732
  239.4 236.3 %copy-start.5 = (s32[16,2048]{1,0:T(8,128)S(1)}, s32[16,2048]{1,0:T(8,128)}, u32[]{:S(2)}) copy-start(s32[16,2048]{1,0:T(8,128)} %copy-done.4) | copy-start | bytes 393220
  253.5 220.5 %all-reduce.11.cloned.1.call-start = ((), (), s32[]{:S(2)}) async-start(), calls=%async_computation.9 | async-start | bytes 2097152 | tf_op jit(solution)/shard_map/psum | solution.py:12
  326.5 230.1 %all-gather.9.cloned.1.call-start = ((), (), s32[]{:S(2)}) async-start(), calls=%async_computation.5 | async-start | bytes 4456448 | tf_op jit(solution)/shard_map/all_gather | solution.py:49
  498.8 99.3 %all-gather.11.cloned.1.call-start = ((), (), s32[]{:S(2)}) async-start(), calls=%async_computation.6 | async-start | bytes 2359296 | tf_op jit(solution)/shard_map/all_gather | solution.py:54
  558.3 143.6 %reduce-scatter.5.cloned.1.call-start = ((), (), s32[]{:S(2)}) async-start(), calls=%async_computation.7 | async-start | bytes 4456448 | tf_op jit(solution)/shard_map/reduce_scatter | solution.py:55
  617.5 90.2 %copy-start.6 = (s32[16,2048]{1,0:T(8,128)S(1)}, s32[16,2048]{1,0:T(8,128)}, u32[]{:S(2)}) copy-start(s32[16,2048]{1,0:T(8,128)} %copy-done.4) | copy-start | bytes 393220
  617.5 176.1 %all-reduce.13.cloned.1.call-start = ((), (), s32[]{:S(2)}) async-start(), calls=%async_computation.10 | async-start | bytes 2097152 | tf_op jit(solution)/shard_map/psum | solution.py:12
  707.5 233.7 %copy-start.1 = (f32[512,1,256]{2,0,1:T(8,128)S(1)}, f32[512,1,256]{2,0,1:T(8,128)}, u32[]{:S(2)}) copy-start(f32[512,1,256]{2,0,1:T(8,128)} %get-tuple-element.7) | copy-start | bytes 1572868
  707.5 233.7 %copy-start.2 = (f32[512,1,256]{2,0,1:T(8,128)S(1)}, f32[512,1,256]{2,0,1:T(8,128)}, u32[]{:S(2)}) copy-start(f32[512,1,256]{2,0,1:T(8,128)} %get-tuple-element.8) | copy-start | bytes 1572868
  720.8 220.4 %all-reduce.9.cloned.1.call-start = ((), (), s32[]{:S(2)}) async-start(), calls=%async_computation.8 | async-start | bytes 2097152 | tf_op jit(solution)/shard_map/psum | solution.py:12
Sparse Core Ops, SparseCore 0:
  31.0 59.5 all-gather.4
  92.5 39.6 all-gather.6
  151.7 84.1 reduce-scatter.2
  253.6 72.8 all-reduce.14
  329.0 144.9 all-reduce.10
  499.0 57.5 all-gather.8
  558.4 39.6 all-gather.10
  617.6 84.1 reduce-scatter.4
  720.9 72.7 all-reduce.12
  796.2 144.9 all-reduce.8
